TPU v7x, 256 devices: a whole 4x4x8 slice. The times are simulated.
256 devices in a mesh: grp: 4 (over y), lst: 64 (over x, z, core).
Axes of the slice: x: 4, y: 4, z: 8, core: 2. Of those that a mesh axis runs over, the one named last changes fastest.
Arguments:
- new_rows: bfloat16 [131072, 1024], P(('grp', 'lst')), may hold values from -6 to 6
- list_ids: int32 [131072], P(('grp', 'lst')), may hold values from 0 to 65535, as said below
- rotation: bfloat16 [1024, 1024], replicated, may hold values from -0.1875 to 0.1875
- centroids: float32 [65536, 1024], P('lst'), may hold values from -6 to 6
- prior_counts: float32 [65536], P('lst'), may hold values from 1 to 10
Outputs:
- new_centroids: float32 [65536, 1024], P('lst')
- residuals: bfloat16 [131072, 1024], P(('grp', 'lst'))
Inputs may be any that keep to these rules, and one draw needn't show every extreme that they name: `list_ids`: on one device, at most 32 rows name lists of one owner (lists o * 1024 to (o + 1) * 1024 - 1); in every draw each group has an owner that gets exactly 32 rows from every device of the group.
All inputs are finite; a program needn't handle non-finite values.
Results may differ from a plain program's by a relative error of at most 0.009.
Values may be sent and summed in bfloat16 or wider, within the bound.
No kernel may reach another device: no remote copies, remote signals or barrier semaphores. Data moves between devices by JAX's collectives and lax.ppermute only.
A program may use at most 128 MiB of HBM per device.

v0:
```python
import jax
import jax.numpy as jnp
from jax import lax
from jax.sharding import PartitionSpec as P


def shards(new_rows, list_ids, rotation, centroids, prior_counts):
    peer_count = lax.axis_size("lst")
    row_count = new_rows.shape[0]
    row_width = new_rows.shape[1]
    per_owner = centroids.shape[0]
    capacity = max(2, 4 * row_count // peer_count)
    owners = list_ids // per_owner
    peer_table = (owners[:, None] == jnp.arange(peer_count, dtype=jnp.int32)[None, :]).astype(
        jnp.int32
    )
    running = jnp.cumsum(peer_table, axis=0) - 1
    slot_rank = jnp.sum(peer_table * running, axis=1)
    dest_index = owners * capacity + slot_rank
    source_row = (
        jnp.full((peer_count * capacity,), row_count, jnp.int32)
        .at[dest_index]
        .set(jnp.arange(row_count, dtype=jnp.int32))
    )
    filled = source_row < row_count
    safe_row = jnp.minimum(source_row, row_count - 1)
    send_rows = jnp.where(
        filled[:, None], jnp.take(new_rows, safe_row, axis=0), jnp.zeros((), jnp.bfloat16)
    ).reshape(peer_count, capacity, row_width)
    send_ids = jnp.where(filled, jnp.take(list_ids, safe_row, axis=0), -1).reshape(
        peer_count, capacity
    )
    list_base = lax.axis_index("lst") * per_owner
    arrived = lax.all_to_all(send_rows, "lst", split_axis=0, concat_axis=0, tiled=True)
    arrived_ids = lax.all_to_all(send_ids, "lst", split_axis=0, concat_axis=0, tiled=True)
    rotated = jnp.einsum(
        "skd,de->ske", arrived, rotation, preferred_element_type=jnp.float32
    ).astype(jnp.bfloat16)
    local_ids = jnp.where(arrived_ids >= 0, arrived_ids - list_base, -1)
    lookup = jnp.take(centroids, jnp.maximum(local_ids, 0), axis=0)
    residual_part = jnp.where(
        (local_ids >= 0)[..., None], rotated.astype(jnp.float32) - lookup, 0.0
    ).astype(jnp.bfloat16)
    residual_buf, local_ids = (residual_part, local_ids)
    flat_res = residual_buf.reshape(-1, row_width)
    flat_ids = local_ids.reshape(-1)
    member = (jnp.arange(per_owner, dtype=jnp.int32)[:, None] == flat_ids[None, :]).astype(
        jnp.bfloat16
    )
    list_sums = jnp.dot(member, flat_res, preferred_element_type=jnp.float32)
    list_counts = jnp.sum(member, axis=1, dtype=jnp.float32)
    total_sums, total_counts = (
        lax.psum(list_sums.astype(jnp.bfloat16), "grp").astype(jnp.float32),
        lax.psum(list_counts.astype(jnp.bfloat16), "grp").astype(jnp.float32),
    )
    new_centroids = centroids + total_sums / (prior_counts + total_counts)[:, None]
    returned = lax.all_to_all(residual_buf, "lst", split_axis=0, concat_axis=0, tiled=True)
    residuals = jnp.take(returned.reshape(-1, row_width), dest_index, axis=0)
    return (new_centroids, residuals)


def solution(mesh):
    return jax.shard_map(
        shards,
        mesh=mesh,
        in_specs=(P(("grp", "lst"), None), P(("grp", "lst")), P(), P("lst", None), P("lst")),
        out_specs=(P("lst", None), P(("grp", "lst"), None)),
        check_vma=False,
    )
```

profile of v0, /device:TPU:1, one launch (start us, length us, event | category | flops | bytes accessed | tf_op | source)
XLA Modules:
  0.0 285.2 jit_solution(8422631312578348476)
XLA Ops:
  7.2 0.0 copy-start
  7.2 0.0 copy-start.1
  7.2 0.8 fusion.16
  8.0 0.7 add_select_fusion
  8.7 1.2 reduce-window.6
  9.9 0.2 slice_reduce_fusion
  10.2 0.1 fusion.7
  10.3 0.7 compare_and_fusion.1
  11.1 2.5 scatter_custom_fusion
  13.5 0.0 copy-done.1
  13.5 0.0 copy-start.2
  13.5 13.2 %gather_fusion = s32[2048]{0:T(1024)S(1)} fusion(s32[512]{0:T(512)S(1)} %copy-done.1, s32[2048]{0:T(1024)S(1)} %fusion.9), kind=kCustom, calls=%fused_computation | custom fusion | bytes 24576 | tf_op jit(solution)/shard_map/jit(_take)/gather | solution.py:30
  26.8 0.7 all_to_all.12
  27.5 13.0 %all-to-all-start = ((s32[64,1,32]{2,1,0:T(1,128)}), s32[64,1,32]{2,1,0:T(1,128)S(1)}, u32[]{:S(2)}, u32[]{:S(2)}) async-start(s32[64,1,32]{2,1,0:T(1,128)} %bitcast.2), calls=%async_computation | async-start | bytes 65536 | tf_op jit(solution)/shard_map/all_to_all | solution.py:35
  40.5 0.1 broadcast_in_dim.91
  40.5 0.1 broadcast_in_dim.89
  40.6 0.0 copy-done.2
  40.6 9.6 %gather_fusion.1 = bf16[2048,1024]{1,0:T(8,128)(2,1)} fusion(bf16[512,1024]{1,0:T(8,128)(2,1)S(1)} %copy-done.2, s32[2048]{0:T(1024)S(1)} %fusion.9), kind=kCustom, calls=%fused_computation.1 | custom fusion | bytes 8396800 | tf_op jit(solution)/shard_map/jit(_take)/gather | solution.py:28
  50.2 4.0 %select_select_fusion = bf16[64,32,1024]{2,1,0:T(8,128)(2,1)} fusion(bf16[64,32,1024]{2,1,0:T(8,128)(2,1)} %bitcast.36, pred[64,32]{1,0:T(8,128)(4,1)S(1)} %broadcast_in_dim.91, pred[64,32]{1,0:T(8,128)(4,1)S(1)} %broadcast_in_dim.89), kind=kLoop, calls=%fused_computation.11 | loop fusion | flops 4194304 | bytes 8392704 | tf_op jit(solution)/shard_map/jit(_where)/select_n | solution.py:27
  54.2 0.0 all-to-all-done
  54.2 10.5 %all-to-all-start.1 = ((bf16[64,32,1024]{2,1,0:T(8,128)(2,1)}), bf16[64,32,1024]{2,1,0:T(8,128)(2,1)}, u32[]{:S(2)}, u32[]{:S(2)}) async-start(bf16[64,32,1024]{2,1,0:T(8,128)(2,1)} %select_select_fusion), calls=%async_computation.1 | async-start | bytes 8388608 | tf_op jit(solution)/shard_map/all_to_all | solution.py:34
  64.7 0.1 copy.20
  64.8 0.1 copy.23
  64.9 0.1 copy.24
  65.1 0.1 copy.25
  65.1 0.1 reshape.149
  65.2 13.9 %gather_fusion.2 = f32[2048,1024]{1,0:T(8,128)} fusion(f32[1024,1024]{1,0:T(8,128)} %param.8, s32[2048]{0:T(1024)S(1)} %broadcast_clamp_fusion), kind=kCustom, calls=%fused_computation.2 | custom fusion | bytes 16785408 | tf_op jit(solution)/shard_map/jit(_take)/gather | solution.py:40
  79.2 81.5 %all-to-all-done.1 = bf16[64,32,1024]{2,1,0:T(8,128)(2,1)} async-done(((bf16[64,32,1024]{2,1,0:T(8,128)(2,1)}), bf16[64,32,1024]{2,1,0:T(8,128)(2,1)}, u32[]{:S(2)}, u32[]{:S(2)}) %all-to-all-start.1) | async-done | bytes 4194336 | tf_op jit(solution)/shard_map/all_to_all | solution.py:34
  160.6 0.0 copy-done
  160.6 9.3 %select_convert_fusion = bf16[64,32,1024]{2,1,0:T(8,128)(2,1)} fusion(f32[64,32,1024]{2,1,0:T(8,128)} %bitcast.37, pred[64,32]{1,0:T(8,128)(4,1)S(1)} %copy.24, pred[64,32]{1,0:T(8,128)(4,1)S(1)} %copy.23, bf16[64,32,1024]{2,1,0:T(8,128)(2,1)} %all-to-all-done.1, bf16[1024,1024]{1,0:T(8,128)(2,1)S(1)} %copy-done), kind=kOutput, calls=%fused_computation.5 | convolution fusion | flops 4307550208 | bytes 18878464 | tf_op jit(solution)/shard_map/skd,de->ske/dot_general | solution.py:36
  169.9 5.9 %all-to-all-start.2 = ((bf16[64,32,1024]{2,1,0:T(8,128)(2,1)}), bf16[64,32,1024]{2,1,0:T(8,128)(2,1)}, u32[]{:S(2)}, u32[]{:S(2)}) async-start(bf16[64,32,1024]{2,1,0:T(8,128)(2,1)} %select_convert_fusion), calls=%async_computation.2 | async-start | bytes 8388608 | tf_op jit(solution)/shard_map/all_to_all | solution.py:57
  175.9 0.0 all-reduce.2.cloned.1.call-start
  175.9 0.1 copy.22
  176.0 0.1 select_n.81
  176.1 0.0 copy-start.3
  176.1 7.9 %fusion.5 = bf16[1024,1024]{1,0:T(8,128)(2,1)} fusion(bf16[2048,1024]{1,0:T(8,128)(2,1)} %bitcast.38, s32[2048]{0:T(1024)S(1)} %select_n.81), kind=kOutput, calls=%fused_computation.14 | convolution fusion | flops 4298113024 | bytes 6299648 | tf_op jit(solution)/shard_map/dot_general | solution.py:50
  183.9 0.0 all-reduce.2.cloned.1.call-update
  184.0 0.9 fusion.2
  184.9 9.7 %psum.15 = bf16[1024]{0:T(1024)(128)(2,1)S(1)} all-reduce(bf16[1024]{0:T(1024)(128)(2,1)S(1)} %fusion.2), channel_id=1, replica_groups=mesh['grp'=4,'lst'=64] {'grp'}, use_global_device_ids=true, to_apply=%region_6.7 | all-reduce | flops 1024 | bytes 4096 | tf_op jit(solution)/shard_map/psum | solution.py:54
  194.6 0.0 copy-done.3
  194.6 54.5 %all-reduce.2.cloned.1.call-done = bf16[1024,1024]{1,0:T(8,128)(2,1)} async-done(((bf16[1024,1024]{1,0:T(8,128)(2,1)}), bf16[1024,1024]{1,0:T(8,128)(2,1)}) %all-reduce.2.cloned.1.call-update) | async-done | bytes 2097168 | tf_op jit(solution)/shard_map/psum | solution.py:53
  249.1 5.9 %divide_add_fusion = f32[1024,1024]{1,0:T(8,128)} fusion(f32[1024,1024]{1,0:T(8,128)} %param.8, bf16[1024,1024]{1,0:T(8,128)(2,1)} %all-reduce.2.cloned.1.call-done, f32[1024]{0:T(1024)S(1)} %convert_add_fusion), kind=kLoop, calls=%fused_computation.10 | loop fusion | flops 3145728 | bytes 10489856 | tf_op jit(solution)/shard_map/add | solution.py:56
  255.0 16.7 %all-to-all-done.2 = bf16[64,32,1024]{2,1,0:T(8,128)(2,1)} async-done(((bf16[64,32,1024]{2,1,0:T(8,128)(2,1)}), bf16[64,32,1024]{2,1,0:T(8,128)(2,1)}, u32[]{:S(2)}, u32[]{:S(2)}) %all-to-all-start.2) | async-done | bytes 4194336 | tf_op jit(solution)/shard_map/all_to_all | solution.py:57
  271.8 5.5 %gather_fusion.3 = bf16[512,1024]{1,0:T(8,128)(2,1)S(1)} fusion(bf16[2048,1024]{1,0:T(8,128)(2,1)} %bitcast.9, s32[1024]{0:T(1024)S(1)} %pad_clamp_fusion), kind=kCustom, calls=%fused_computation.3 | custom fusion | bytes 2099200 | tf_op jit(solution)/shard_map/jit(_take)/gather | solution.py:58
  277.2 1.1 broadcast_select_fusion
  (12 shorter events, 0.1 us)
Async XLA Ops:
  7.2 153.5 %copy-start = (bf16[1024,1024]{1,0:T(8,128)(2,1)S(1)}, bf16[1024,1024]{1,0:T(8,128)(2,1)}, u32[]{:S(2)}) copy-start(bf16[1024,1024]{1,0:T(8,128)(2,1)} %param.7) | copy-start | bytes 6291460
  7.2 6.4 %copy-start.1 = (s32[512]{0:T(512)S(1)}, s32[512]{0:T(512)}, u32[]{:S(2)}) copy-start(s32[512]{0:T(512)} %param.6) | copy-start | bytes 6148
  13.5 27.1 %copy-start.2 = (bf16[512,1024]{1,0:T(8,128)(2,1)S(1)}, bf16[512,1024]{1,0:T(8,128)(2,1)}, u32[]{:S(2)}) copy-start(bf16[512,1024]{1,0:T(8,128)(2,1)} %param.5) | copy-start | bytes 3145732
  27.5 26.7 %all-to-all-start = ((s32[64,1,32]{2,1,0:T(1,128)}), s32[64,1,32]{2,1,0:T(1,128)S(1)}, u32[]{:S(2)}, u32[]{:S(2)}) async-start(s32[64,1,32]{2,1,0:T(1,128)} %bitcast.2), calls=%async_computation | async-start | bytes 65536 | tf_op jit(solution)/shard_map/all_to_all | solution.py:35
  54.2 106.4 %all-to-all-start.1 = ((bf16[64,32,1024]{2,1,0:T(8,128)(2,1)}), bf16[64,32,1024]{2,1,0:T(8,128)(2,1)}, u32[]{:S(2)}, u32[]{:S(2)}) async-start(bf16[64,32,1024]{2,1,0:T(8,128)(2,1)} %select_select_fusion), calls=%async_computation.1 | async-start | bytes 8388608 | tf_op jit(solution)/shard_map/all_to_all | solution.py:34
  169.9 101.8 %all-to-all-start.2 = ((bf16[64,32,1024]{2,1,0:T(8,128)(2,1)}), bf16[64,32,1024]{2,1,0:T(8,128)(2,1)}, u32[]{:S(2)}, u32[]{:S(2)}) async-start(bf16[64,32,1024]{2,1,0:T(8,128)(2,1)} %select_convert_fusion), calls=%async_computation.2 | async-start | bytes 8388608 | tf_op jit(solution)/shard_map/all_to_all | solution.py:57
  175.9 73.2 %all-reduce.2.cloned.1.call-start = ((), (), s32[]{:S(2)}) async-start(), calls=%async_computation.3 | async-start | bytes 4194304 | tf_op jit(solution)/shard_map/psum | solution.py:53
  176.1 18.5 %copy-start.3 = (f32[1024]{0:T(1024)S(1)}, f32[1024]{0:T(1024)}, u32[]{:S(2)}) copy-start(f32[1024]{0:T(1024)} %param.9) | copy-start | bytes 12292
Sparse Core Ops, SparseCore 0:
  184.1 64.9 all-reduce.1
where the time goes:
time: 286 us; the launch traced here: 285 us
  waiting for transfers between devices  153 us (53%)
  local copies, waits for them, and re-layouts  46.4 us (16%)
  starting transfers between devices  29.5 us (10%)
  matrix products  17.2 us (6%)
  other arithmetic  15.6 us (5%)
  between operations  14.2 us (5%)
  blocking collectives  9.72 us (3%)
    all_to_all x1, waiting for transfers between devices, shards(): lax.all_to_all(send_rows, 'lst', split_axis=0, concat_axis=0, tiled=True)  81.5 us
    psum x1, waiting for transfers between devices, shards(): lax.psum(list_sums.astype(jnp.bfloat16), 'grp').astype(jnp.float32)  54.5 us
    all_to_all x1, waiting for transfers between devices, shards(): lax.all_to_all(residual_buf, 'lst', split_axis=0, concat_axis=0, tiled=True)  16.7 us
    gather x1, local copies, waits for them, and re-layouts, shards(): lookup = jnp.take(centroids, jnp.maximum(local_ids, 0), axis=0)  13.9 us
    gather x1, local copies, waits for them, and re-layouts, shards(): jnp.take(list_ids, safe_row, axis=0)  13.2 us
    all_to_all x1, starting transfers between devices, shards(): lax.all_to_all(send_ids, 'lst', split_axis=0, concat_axis=0, tiled=True)  13 us
    all_to_all x1, starting transfers between devices, shards(): lax.all_to_all(send_rows, 'lst', split_axis=0, concat_axis=0, tiled=True)  10.5 us
    psum x1, blocking collectives, shards(): lax.psum(list_counts.astype(jnp.bfloat16), 'grp').astype(jnp.float32)  9.72 us
  transfers between devices with their start and end apart: 4, of which 3 were waited for; matrix products, arithmetic and copies ran while one was open for 15% of the time, Pallas kernels for 0%

commit v1 on v0

v1 whole, which is shorter than its diff:
```python
import functools

import jax
import jax.numpy as jnp
from jax import lax
from jax.experimental import pallas as pl
from jax.experimental.pallas import tpu as pltpu
from jax.sharding import PartitionSpec as P

CONTRACT_LAST = (((1,), (1,)), ((), ()))
CONTRACT_FIRST = (((0,), (0,)), ((), ()))
BF16 = jnp.bfloat16
F32 = jnp.float32


def slots_kernel(peers, capacity, per_owner, ids_ref, slot_ref, codes_ref):
    ids = ids_ref[...]
    rows = ids.shape[1]
    owner = ids // per_owner
    local = ids - owner * per_owner + 1
    member = lax.broadcasted_iota(jnp.int32, (peers, rows), 0) == owner
    member_f = jnp.where(member, 1.0, 0.0).astype(F32)
    earlier = lax.broadcasted_iota(jnp.int32, (rows, rows), 0) < lax.broadcasted_iota(
        jnp.int32, (rows, rows), 1
    )
    before = jnp.dot(
        member_f.astype(BF16),
        jnp.where(earlier, 1.0, 0.0).astype(BF16),
        preferred_element_type=F32,
    )
    rank = jnp.sum(jnp.where(member, before, 0.0), axis=0, keepdims=True).astype(jnp.int32)
    slot_ref[...] = owner * capacity + rank
    at_rank = lax.broadcasted_iota(jnp.int32, (capacity, rows), 0) == rank
    at_rank = jnp.where(at_rank, 1.0, 0.0).astype(BF16)
    high = local // 32
    low = local - high * 32

    def place(value):
        spread = jnp.where(member, value.astype(F32), 0.0).astype(BF16)
        return lax.dot_general(spread, at_rank, CONTRACT_LAST, preferred_element_type=F32)

    codes_ref[...] = (place(high) * 32.0 + place(low)).astype(jnp.int32)


def pack_kernel(block, slot_ref, rows_ref, rotation_ref, send_ref, rotated_ref):
    step = pl.program_id(0)

    @pl.when(step == 0)
    def _():
        rotated_ref[...] = jnp.dot(
            rows_ref[...], rotation_ref[...], preferred_element_type=F32
        ).astype(BF16)

    rows = rows_ref.shape[0]
    chosen = lax.broadcasted_iota(jnp.int32, (block, rows), 0) + step * block == slot_ref[...]
    send_ref[...] = jnp.dot(
        jnp.where(chosen, 1.0, 0.0).astype(BF16), rotated_ref[...], preferred_element_type=F32
    ).astype(BF16)


def unpack_kernel(slot_ref, returned_ref, out_ref, chosen_ref):
    slots, rows = chosen_ref.shape

    @pl.when(pl.program_id(0) == 0)
    def _():
        chosen = lax.broadcasted_iota(jnp.int32, (slots, rows), 0) == slot_ref[...]
        chosen_ref[...] = jnp.where(chosen, 1.0, 0.0).astype(BF16)

    out_ref[...] = lax.dot_general(
        chosen_ref[...], returned_ref[...], CONTRACT_FIRST, preferred_element_type=F32
    ).astype(BF16)


def whole(shape):
    return pl.BlockSpec(shape, lambda i: (0,) * len(shape))


def make_slots(list_ids, peers, capacity, per_owner):
    rows = list_ids.shape[0]
    return pl.pallas_call(
        functools.partial(slots_kernel, peers, capacity, per_owner),
        out_shape=(
            jax.ShapeDtypeStruct((1, rows), jnp.int32),
            jax.ShapeDtypeStruct((peers, capacity), jnp.int32),
        ),
        name="slots",
    )(list_ids.reshape(1, rows))


def pack(slot, new_rows, rotation, slots):
    rows, width = new_rows.shape
    block = 256
    return pl.pallas_call(
        functools.partial(pack_kernel, block),
        grid=(slots // block,),
        in_specs=[whole(slot.shape), whole(new_rows.shape), whole(rotation.shape)],
        out_specs=pl.BlockSpec((block, width), lambda i: (i, 0)),
        out_shape=jax.ShapeDtypeStruct((slots, width), BF16),
        scratch_shapes=[pltpu.VMEM((rows, width), BF16)],
        compiler_params=pltpu.CompilerParams(vmem_limit_bytes=40 * 2**20),
        name="pack",
    )(slot, new_rows, rotation)


def unpack(slot, returned):
    rows = slot.shape[1]
    slots, width = returned.shape
    block = 256
    return pl.pallas_call(
        unpack_kernel,
        grid=(width // block,),
        in_specs=[whole(slot.shape), pl.BlockSpec((slots, block), lambda i: (0, i))],
        out_specs=pl.BlockSpec((rows, block), lambda i: (0, i)),
        out_shape=jax.ShapeDtypeStruct((rows, width), BF16),
        scratch_shapes=[pltpu.VMEM((slots, rows), BF16)],
        compiler_params=pltpu.CompilerParams(vmem_limit_bytes=40 * 2**20),
        name="unpack",
    )(slot, returned)


def shards(new_rows, list_ids, rotation, centroids, prior_counts):
    peers = lax.axis_size("lst")
    row_count, width = new_rows.shape
    per_owner = centroids.shape[0]
    capacity = max(2, 4 * row_count // peers)
    slots = peers * capacity
    slot, codes = make_slots(list_ids, peers, capacity, per_owner)
    arrived_codes = lax.all_to_all(codes, "lst", split_axis=0, concat_axis=0, tiled=True)
    send_rows = pack(slot, new_rows, rotation, slots).reshape(peers, capacity, width)
    arrived = lax.all_to_all(send_rows, "lst", split_axis=0, concat_axis=0, tiled=True)
    local = arrived_codes.reshape(slots) - 1
    lookup = jnp.take(centroids, jnp.maximum(local, 0), axis=0)
    residual = jnp.where(
        (local >= 0)[:, None], arrived.reshape(slots, width).astype(F32) - lookup, 0.0
    ).astype(BF16)
    returned = lax.all_to_all(
        residual.reshape(peers, capacity, width), "lst", split_axis=0, concat_axis=0, tiled=True
    )
    member = (jnp.arange(per_owner, dtype=jnp.int32)[:, None] == local[None, :]).astype(BF16)
    list_sums = jnp.dot(member, residual, preferred_element_type=F32)
    list_counts = jnp.sum(member, axis=1, dtype=F32)
    total_sums = lax.psum(list_sums.astype(BF16), "grp").astype(F32)
    total_counts = lax.psum(list_counts, "grp")
    new_centroids = centroids + total_sums / (prior_counts + total_counts)[:, None]
    residuals = unpack(slot, returned.reshape(slots, width))
    return (new_centroids, residuals)


def solution(mesh):
    return jax.shard_map(
        shards,
        mesh=mesh,
        in_specs=(P(("grp", "lst"), None), P(("grp", "lst")), P(), P("lst", None), P("lst")),
        out_specs=(P("lst", None), P(("grp", "lst"), None)),
        check_vma=False,
    )
```

time: 286 us -> 261 us (0.913)
  local copies, waits for them, and re-layouts: 46.4 us -> 20.1 us
  Pallas kernels: 0 us -> 12.5 us
  matrix products: 17.2 us -> 5.74 us
  other arithmetic: 15.6 us -> 19.1 us
  waiting for transfers between devices: 153 us -> 150 us
    gather x4 -> x1, local copies, waits for them, and re-layouts: 42.2 us -> 14 us  [shards(): lookup = jnp.take(centroids, jnp.maximum(local, 0), axis=0)]
    pallas_call x0 -> x3, Pallas kernels: none -> 12.5 us  [the longest x1 6 us: unpack(): pl.pallas_call(unpack_kernel, grid=(width // block,), in_specs=[whole(slo...]
    convert_element_type x1 -> x2, other arithmetic: 0.01 us -> 12.2 us  [shards(): residual = jnp.where((local >= 0)[:, None], arrived.reshape(slots, width)...]
    dot_general x2 -> x1, matrix products: 17.2 us -> 5.74 us  [shards(): list_sums = jnp.dot(member, residual, preferred_element_type=F32)]
    select_n x4 -> x0, other arithmetic: 5.8 us -> none  [the longest x1 3.97 us: shards(): jnp.where(filled[:, None], jnp.take(new_rows, safe_row, axis=0), jnp.zero...]
    unnamed x8 -> x12, local copies, waits for them, and re-layouts: 0.03 us -> 5.51 us
    all_to_all x2, waiting for transfers between devices: 16.7 us -> 13.4 us  [the longest x1 13.4 us: shards(): lax.all_to_all(residual.reshape(peers, capacity, width), 'lst', split_axi...]
  transfers between devices with their start and end apart: 4 -> 4, of which waited for: 3 -> 3; matrix products, arithmetic and copies ran while one was open for 15% -> 13% of each run, Pallas kernels for 0% -> 2%
where the time goes in v1:
time: 261 us; the launch traced here: 260 us
  waiting for transfers between devices  150 us (57%)
  starting transfers between devices  29.5 us (11%)
  local copies, waits for them, and re-layouts  20.1 us (8%)
  other arithmetic  19.1 us (7%)
  between operations  14.1 us (5%)
  Pallas kernels  12.5 us (5%)
  blocking collectives  9.53 us (4%)
  matrix products  5.74 us (2%)
    all_to_all x1, waiting for transfers between devices, shards(): lax.all_to_all(send_rows, 'lst', split_axis=0, concat_axis=0, tiled=True)  81.4 us
    psum x1, waiting for transfers between devices, shards(): total_sums = lax.psum(list_sums.astype(BF16), 'grp').astype(F32)  54.7 us
    gather x1, local copies, waits for them, and re-layouts, shards(): lookup = jnp.take(centroids, jnp.maximum(local, 0), axis=0)  14 us
    all_to_all x1, waiting for transfers between devices, shards(): lax.all_to_all(residual.reshape(peers, capacity, width), 'lst', split_axi...  13.4 us
    all_to_all x1, starting transfers between devices, shards(): lax.all_to_all(codes, 'lst', split_axis=0, concat_axis=0, tiled=True)  13 us
    convert_element_type x2, other arithmetic, shards(): residual = jnp.where((local >= 0)[:, None], arrived.reshape(slots, width)...  12.2 us
    all_to_all x1, starting transfers between devices, shards(): lax.all_to_all(send_rows, 'lst', split_axis=0, concat_axis=0, tiled=True)  10.5 us
    psum x1, blocking collectives, shards(): total_counts = lax.psum(list_counts, 'grp')  9.53 us
  transfers between devices with their start and end apart: 4, of which 3 were waited for; matrix products, arithmetic and copies ran while one was open for 13% of the time, Pallas kernels for 2%

profile of v1, /device:TPU:1, one launch (start us, length us, event | category | flops | bytes accessed | tf_op | source)
XLA Modules:
  0.0 260.1 jit_solution(13835307723788588174)
XLA Ops:
  7.2 1.7 slots.1
  8.9 13.0 %all-to-all-start = ((s32[64,1,32]{2,1,0:T(1,128)}), s32[64,1,32]{2,1,0:T(1,128)S(1)}, u32[]{:S(2)}, u32[]{:S(2)}) async-start(s32[64,1,32]{2,1,0:T(1,128)} %bitcast.24), calls=%async_computation | async-start | bytes 65536 | tf_op jit(solution)/shard_map/all_to_all | solution.py:128
  21.9 0.0 copy-start.1
  21.9 1.6 copy-done.1
  23.4 0.0 copy-start.2
  23.5 1.2 copy-done.2
  24.7 0.0 copy-start.3
  24.7 0.7 copy-done.3
  25.4 4.8 %pack.1 = bf16[2048,1024]{1,0:T(8,128)(2,1)S(1)} custom-call(s32[1,512]{1,0:T(1,128)S(1)} %copy-done.3, bf16[512,1024]{1,0:T(8,128)(2,1)S(1)} %copy-done.2, bf16[1024,1024]{1,0:T(8,128)(2,1)S(1)} %copy-done.1), custom_call_target="tpu_custom_call" | custom-call | tf_op jit(solution)/shard_map/pack/pallas_call | solution.py:93
  30.2 0.0 copy-start
  30.2 2.0 copy-done
  32.2 0.0 all-to-all-done
  32.2 10.5 %all-to-all-start.1 = ((bf16[64,32,1024]{2,1,0:T(8,128)(2,1)}), bf16[64,32,1024]{2,1,0:T(8,128)(2,1)}, u32[]{:S(2)}, u32[]{:S(2)}) async-start(bf16[64,32,1024]{2,1,0:T(8,128)(2,1)} %bitcast.22), calls=%async_computation.1 | async-start | bytes 8388608 | tf_op jit(solution)/shard_map/all_to_all | solution.py:130
  42.7 0.1 copy.15
  42.8 0.1 copy.18
  42.9 0.1 copy.19
  43.0 0.1 copy.17
  43.1 0.1 reshape.85
  43.2 14.0 %gather_fusion = f32[2048,1024]{1,0:T(8,128)} fusion(f32[1024,1024]{1,0:T(8,128)} %param.8, s32[2048]{0:T(1024)S(1)} %broadcast_clamp_fusion), kind=kCustom, calls=%fused_computation | custom fusion | bytes 16785408 | tf_op jit(solution)/shard_map/jit(_take)/gather | solution.py:132
  57.2 81.4 %all-to-all-done.1 = bf16[64,32,1024]{2,1,0:T(8,128)(2,1)} async-done(((bf16[64,32,1024]{2,1,0:T(8,128)(2,1)}), bf16[64,32,1024]{2,1,0:T(8,128)(2,1)}, u32[]{:S(2)}, u32[]{:S(2)}) %all-to-all-start.1) | async-done | bytes 4194336 | tf_op jit(solution)/shard_map/all_to_all | solution.py:130
  138.6 6.8 %select_convert_fusion = bf16[64,32,1024]{2,1,0:T(8,128)(2,1)} fusion(f32[64,32,1024]{2,1,0:T(8,128)} %bitcast.23, pred[64,32]{1,0:T(8,128)(4,1)S(1)} %copy.19, pred[64,32]{1,0:T(8,128)(4,1)S(1)} %copy.18, bf16[64,32,1024]{2,1,0:T(8,128)(2,1)} %all-to-all-done.1), kind=kLoop, calls=%fused_computation.4 | loop fusion | flops 10485760 | bytes 16781312 | tf_op jit(solution)/shard_map/convert_element_type | solution.py:135
  145.4 5.9 %all-to-all-start.2 = ((bf16[64,32,1024]{2,1,0:T(8,128)(2,1)}), bf16[64,32,1024]{2,1,0:T(8,128)(2,1)}, u32[]{:S(2)}, u32[]{:S(2)}) async-start(bf16[64,32,1024]{2,1,0:T(8,128)(2,1)} %select_convert_fusion), calls=%async_computation.2 | async-start | bytes 8388608 | tf_op jit(solution)/shard_map/all_to_all | solution.py:136
  151.3 0.0 all-reduce.2.cloned.1.call-start
  151.4 0.1 copy.16
  151.5 0.1 sub.13
  151.6 5.4 %fusion.1 = bf16[2048,1024]{1,0:T(8,128)(2,1)S(1)} fusion(f32[2048,1024]{1,0:T(8,128)} %gather_fusion, pred[2048]{0:T(1024)(128)(4,1)S(1)} %get-tuple-element.11, pred[2048]{0:T(1024)(128)(4,1)S(1)} %get-tuple-element.10, bf16[64,32,1024]{2,1,0:T(8,128)(2,1)} %all-to-all-done.1), kind=kLoop, calls=%fused_computation.3 | loop fusion | flops 10485760 | bytes 16781312 | tf_op jit(solution)/shard_map/convert_element_type | solution.py:135
  157.0 0.0 copy-start.5
  157.0 5.7 %fusion.5 = bf16[1024,1024]{1,0:T(8,128)(2,1)} fusion(bf16[2048,1024]{1,0:T(8,128)(2,1)S(1)} %fusion.1, s32[2048]{0:T(1024)S(1)} %sub.13), kind=kOutput, calls=%fused_computation.11 | convolution fusion | flops 4298113024 | bytes 6299648 | tf_op jit(solution)/shard_map/dot_general | solution.py:140
  162.7 0.0 all-reduce.2.cloned.1.call-update
  162.8 0.9 convert_reduce_fusion
  163.7 9.5 %psum.15 = f32[1024]{0:T(1024)S(1)} all-reduce(f32[1024]{0:T(1024)S(1)} %convert_reduce_fusion), channel_id=1, replica_groups=mesh['grp'=4,'lst'=64] {'grp'}, use_global_device_ids=true, to_apply=%region_2.3 | all-reduce | flops 1024 | bytes 8192 | tf_op jit(solution)/shard_map/psum | solution.py:143
  173.2 0.0 copy-done.5
  173.2 0.0 copy-start.4
  173.2 54.7 %all-reduce.2.cloned.1.call-done = bf16[1024,1024]{1,0:T(8,128)(2,1)} async-done(((bf16[1024,1024]{1,0:T(8,128)(2,1)}), bf16[1024,1024]{1,0:T(8,128)(2,1)}) %all-reduce.2.cloned.1.call-update) | async-done | bytes 2097168 | tf_op jit(solution)/shard_map/psum | solution.py:142
  227.9 5.9 %divide_add_fusion = f32[1024,1024]{1,0:T(8,128)} fusion(f32[1024,1024]{1,0:T(8,128)} %param.8, bf16[1024,1024]{1,0:T(8,128)(2,1)} %all-reduce.2.cloned.1.call-done, f32[1024]{0:T(1024)S(1)} %add.36), kind=kLoop, calls=%fused_computation.9 | loop fusion | flops 3145728 | bytes 10489856 | tf_op jit(solution)/shard_map/add | solution.py:144
  233.8 13.4 %all-to-all-done.2 = bf16[64,32,1024]{2,1,0:T(8,128)(2,1)} async-done(((bf16[64,32,1024]{2,1,0:T(8,128)(2,1)}), bf16[64,32,1024]{2,1,0:T(8,128)(2,1)}, u32[]{:S(2)}, u32[]{:S(2)}) %all-to-all-start.2) | async-done | bytes 4194336 | tf_op jit(solution)/shard_map/all_to_all | solution.py:136
  247.2 0.0 copy-done.4
  247.2 6.0 %unpack.1 = bf16[512,1024]{1,0:T(8,128)(2,1)} custom-call(s32[1,512]{1,0:T(1,128)S(1)} %copy-done.4, bf16[2048,1024]{1,0:T(8,128)(2,1)} %bitcast.8.returned_ref), custom_call_target="tpu_custom_call" | custom-call | tf_op jit(solution)/shard_map/unpack/pallas_call | solution.py:109
  (5 shorter events, 0.0 us)
Async XLA Ops:
  8.9 23.4 %all-to-all-start = ((s32[64,1,32]{2,1,0:T(1,128)}), s32[64,1,32]{2,1,0:T(1,128)S(1)}, u32[]{:S(2)}, u32[]{:S(2)}) async-start(s32[64,1,32]{2,1,0:T(1,128)} %bitcast.24), calls=%async_computation | async-start | bytes 65536 | tf_op jit(solution)/shard_map/all_to_all | solution.py:128
  21.9 1.6 copy-start.1
  23.4 1.2 copy-start.2
  24.7 0.7 copy-start.3
  30.2 2.0 copy-start
  32.2 106.4 %all-to-all-start.1 = ((bf16[64,32,1024]{2,1,0:T(8,128)(2,1)}), bf16[64,32,1024]{2,1,0:T(8,128)(2,1)}, u32[]{:S(2)}, u32[]{:S(2)}) async-start(bf16[64,32,1024]{2,1,0:T(8,128)(2,1)} %bitcast.22), calls=%async_computation.1 | async-start | bytes 8388608 | tf_op jit(solution)/shard_map/all_to_all | solution.py:130
  145.4 101.8 %all-to-all-start.2 = ((bf16[64,32,1024]{2,1,0:T(8,128)(2,1)}), bf16[64,32,1024]{2,1,0:T(8,128)(2,1)}, u32[]{:S(2)}, u32[]{:S(2)}) async-start(bf16[64,32,1024]{2,1,0:T(8,128)(2,1)} %select_convert_fusion), calls=%async_computation.2 | async-start | bytes 8388608 | tf_op jit(solution)/shard_map/all_to_all | solution.py:136
  151.3 76.5 %all-reduce.2.cloned.1.call-start = ((), (), s32[]{:S(2)}) async-start(), calls=%async_computation.3 | async-start | bytes 4194304 | tf_op jit(solution)/shard_map/psum | solution.py:142
  157.0 16.2 %copy-start.5 = (f32[1024]{0:T(1024)S(1)}, f32[1024]{0:T(1024)}, u32[]{:S(2)}) copy-start(f32[1024]{0:T(1024)} %param.9) | copy-start | bytes 12292
  173.2 74.0 %copy-start.4 = (s32[1,512]{1,0:T(1,128)S(1)}, s32[1,512]{1,0:T(1,128)}, u32[]{:S(2)}) copy-start(s32[1,512]{1,0:T(1,128)} %get-tuple-element.5.slot_ref) | copy-start | bytes 6148
Sparse Core Ops, SparseCore 0:
  162.9 64.9 all-reduce.1
